TPU v7x, 32 devices: a whole 2x2x4 slice. The times are simulated.
32 devices in a mesh: row: 4 (over z), col: 8 (over y, x, core).
Axes of the slice: x: 2, y: 2, z: 4, core: 2. Of those that a mesh axis runs over, the one named last changes fastest.
Arguments:
- gradient: bfloat16 [8192, 8192], P('row', 'col'), may hold values from -1.5 to 1.5
- stat_old: float32 [8192, 8192], P('row', 'col'), may hold values from -6 to 6
- inv_root: bfloat16 [8192, 8192], P('row'), may hold values from -0.0625 to 0.0625
Outputs:
- stat_new: float32 [8192, 8192], P('row', 'col')
- preconditioned: bfloat16 [8192, 8192], P('row', 'col')
All inputs are finite; a program needn't handle non-finite values.
Results may differ from a plain program's by a relative error of at most 0.012.
Values may be sent and summed in bfloat16 or wider, within the bound.
A program may use at most 192 MiB of HBM per device.

v0:
```python
import jax
import jax.numpy as jnp
from jax import lax
from jax.sharding import PartitionSpec as P


def on_device(gradient, stat_old, inv_root):
    columns = lax.all_gather(gradient, "row", axis=0, tiled=True)
    shares = lax.psum_scatter(
        lax.dot_general(
            columns, gradient, (((1,), (1,)), ((), ())), preferred_element_type=jnp.float32
        ).astype(jnp.bfloat16),
        "col",
        scatter_dimension=0,
        tiled=True,
    ).astype(jnp.float32)
    tile = shares.T
    stat_new = 0.9 * stat_old + 0.1 * tile
    product = jnp.dot(inv_root, columns, preferred_element_type=jnp.float32)
    return (stat_new, product.astype(jnp.bfloat16))


def solution(mesh):
    placed = (P("row", "col"), P("row", "col"), P("row", None))
    return jax.shard_map(
        on_device,
        mesh=mesh,
        in_specs=placed,
        out_specs=(P("row", "col"), P("row", "col")),
        check_vma=False,
    )
```

profile of v0, /device:TPU:2, one launch (start us, length us, event | category | flops | bytes accessed | tf_op | source)
XLA Modules:
  0.0 572.5 jit_solution(11946630468866113314)
XLA Ops:
  7.2 0.0 all-gather.2.cloned.1.call-start
  7.2 0.7 all-gather.2.cloned.1.call-update
  7.9 0.0 reduce-scatter.2.cloned.1.call-start
  7.9 289.7 %all-gather.2.cloned.1.call-done = bf16[8192,1024]{1,0:T(8,128)(2,1)} async-done(((bf16[2048,1024]{1,0:T(8,128)(2,1)}), bf16[8192,1024]{1,0:T(8,128)(2,1)}) %all-gather.2.cloned.1.call-update) | async-done | bytes 16777232 | tf_op jit(solution)/shard_map/all_gather | solution.py:8
  297.6 45.2 %convolution_convert_fusion = bf16[8192,2048]{1,0:T(8,128)(2,1)} fusion(bf16[8192,1024]{1,0:T(8,128)(2,1)} %all-gather.2.cloned.1.call-done, bf16[2048,1024]{1,0:T(8,128)(2,1)} %param.3), kind=kOutput, calls=%fused_computation | convolution fusion | flops 34376515584 | bytes 54525952 | tf_op jit(solution)/shard_map/dot_general | solution.py:10
  342.9 0.0 reduce-scatter.2.cloned.1.call-update
  342.9 9.5 %copy.5 = f32[2048,1024]{0,1:T(8,128)} copy(f32[2048,1024]{1,0:T(8,128)} %param.4) | data formatting | bytes 16777216 | tf_op args[1]
  352.4 48.9 %convolution_convert_fusion.1 = bf16[2048,1024]{1,0:T(8,128)(2,1)} fusion(bf16[2048,8192]{1,0:T(8,128)(2,1)} %param.5, bf16[8192,1024]{1,0:T(8,128)(2,1)} %all-gather.2.cloned.1.call-done), kind=kOutput, calls=%fused_computation.2 | convolution fusion | flops 34361835520 | bytes 54525952 | tf_op jit(solution)/shard_map/dot_general | solution.py:19
  401.3 145.1 %reduce-scatter.2.cloned.1.call-done = bf16[1024,2048]{1,0:T(8,128)(2,1)} async-done(((bf16[8192,2048]{1,0:T(8,128)(2,1)}), bf16[1024,2048]{1,0:T(8,128)(2,1)}) %reduce-scatter.2.cloned.1.call-update) | async-done | bytes 4194320 | tf_op jit(solution)/shard_map/reduce_scatter | solution.py:9
  546.3 10.0 %bitcast_add_fusion = f32[2048,1024]{0,1:T(8,128)} fusion(bf16[1024,2048]{1,0:T(8,128)(2,1)} %reduce-scatter.2.cloned.1.call-done, f32[2048,1024]{0,1:T(8,128)} %copy.5), kind=kLoop, calls=%fused_computation.1 | loop fusion | flops 8388608 | bytes 20971520 | tf_op jit(solution)/shard_map/add | solution.py:18
  556.4 9.2 %copy.6 = f32[2048,1024]{1,0:T(8,128)} copy(f32[2048,1024]{0,1:T(8,128)} %bitcast_add_fusion) | data formatting | bytes 16777216
Async XLA Ops:
  7.2 290.4 %all-gather.2.cloned.1.call-start = ((), (), s32[]{:S(2)}) async-start(), calls=%async_computation.1 | async-start | bytes 20971520 | tf_op jit(solution)/shard_map/all_gather | solution.py:8
  7.9 538.5 %reduce-scatter.2.cloned.1.call-start = ((), (), s32[]{:S(2)}) async-start(), calls=%async_computation.2 | async-start | bytes 37748736 | tf_op jit(solution)/shard_map/reduce_scatter | solution.py:9
Sparse Core Ops, SparseCore 0:
  9.6 287.9 all-gather.1
  343.0 203.3 reduce-scatter.1
where the time goes:
time: 574 us; the launch traced here: 572 us
  waiting for transfers between devices  435 us (76%)
  matrix products  94.1 us (16%)
  local copies, waits for them, and re-layouts  18.8 us (3%)
  between operations  14 us (2%)
  other arithmetic  10 us (2%)
    all_gather x1, waiting for transfers between devices, on_device(): columns = lax.all_gather(gradient, 'row', axis=0, tiled=True)  290 us
    reduce_scatter x1, waiting for transfers between devices, on_device(): lax.psum_scatter(lax.dot_general(columns, gradient, (((1,), (1,)), ((), (...  145 us
    dot_general x1, matrix products, on_device(): product = jnp.dot(inv_root, columns, preferred_element_type=jnp.float32)  48.9 us
    dot_general x1, matrix products, on_device(): lax.dot_general(columns, gradient, (((1,), (1,)), ((), ())), preferred_el...  45.2 us
    unnamed x2, local copies, waits for them, and re-layouts  18.8 us
  transfers between devices with their start and end apart: 2, of which 2 were waited for; matrix products, arithmetic and copies ran while one was open for 10% of the time, Pallas kernels for 0%

commit v1 on v0

v1 whole, which is shorter than its diff:
```python
import functools

import jax
import jax.numpy as jnp
from jax import lax
from jax.experimental import pallas as pl
from jax.experimental.pallas import tpu as pltpu
from jax.sharding import PartitionSpec as P

MESH = pl.DeviceIdType.MESH
WIDE = 128
NT = (((1,), (1,)), ((), ()))


def plan(nr):
    units = [(nr - 1, 2), (0, 0)]
    for place in range(1, nr - 1):
        for step in range(2, nr):
            if 2 * (step - 1) % (nr - 1) == place:
                units.append((step - 1, 2 * (step - 1) // (nr - 1)))
    return units


def kernel(nr, nc, m, tile, g_ref, r_ref, share_ref, out_ref, gv, acc, cols, rbuf, part, got, pair, heap, stage,
           zs, zr, rs, ps, pr, ss, sr, ts, ls):
    rows = gv.shape[0]
    sub = rows // 2
    chunks = sub // m
    nq = nc // 2
    z, c = lax.axis_index("row"), lax.axis_index("col")
    q, k = c // 2, c % 2
    right, left = lax.rem(z + 1, nr), lax.rem(z + nr - 1, nr)
    mate = 2 * q + (1 - k)

    barrier = pltpu.get_barrier_semaphore()
    others = [(right, c), (left, c), (z, mate)]
    others += [(z, 2 * lax.rem(q + i, nq) + k) for i in range(1, nq)]
    for other in others:
        pl.semaphore_signal(barrier, inc=1, device_id=other, device_id_type=MESH)
    pl.semaphore_wait(barrier, len(others))

    def at(j):
        return pl.ds(pl.multiple_of(j * m, m), m)

    def ring(j, step):
        src = g_ref.at[:, at(j)] if step == 1 else cols.at[j, step - 2]
        return pltpu.make_async_remote_copy(
            src_ref=src, dst_ref=cols.at[j, step - 1], send_sem=zs.at[j, step - 1], recv_sem=zr.at[j, step - 1],
            device_id=(right, c), device_id_type=MESH)

    def weights(i, step, j, h):
        block = lax.rem(z + nr - step, nr)
        first = pl.multiple_of((2 * block + h) * sub + j * m, m)
        return pltpu.make_async_copy(
            r_ref.at[:, pl.ds(first, m)], rbuf.at[i, :, pl.ds(h * m, m)], rs.at[i, h])

    def swap(i):
        return pltpu.make_async_remote_copy(
            src_ref=part.at[i, 1 - k], dst_ref=got.at[i], send_sem=ps.at[i], recv_sem=pr.at[i],
            device_id=(z, mate), device_id_type=MESH)

    def spread(i, step, j):
        block = lax.rem(z + nr - step, nr)
        return pltpu.make_async_remote_copy(
            src_ref=pair.at[i], dst_ref=heap.at[j, q], send_sem=ss.at[i], recv_sem=sr.at[j, q],
            device_id=(z, 2 * block + k), device_id_type=MESH)

    def store(j):
        return pltpu.make_async_copy(stage.at[j % 2], share_ref.at[:, at(j)], ts.at[j % 2])

    units = plan(nr)
    ring(0, 1).start()
    if chunks > 1:
        ring(1, 1).start()
    whole = [pltpu.make_async_copy(g_ref.at[h], gv.at[pl.ds(h * sub, sub)], ls.at[h]) for h in range(2)]
    for copy in whole:
        copy.start()
    for i, (step, _) in enumerate(units):
        for h in range(2):
            weights(i, step, 0, h).start()

    def clear(t, _):
        acc[pl.ds(pl.multiple_of(t * tile, tile), tile)] = jnp.zeros((tile, acc.shape[1]), jnp.float32)
        return 0

    lax.fori_loop(0, rows // tile, clear, 0)
    for copy in whole:
        copy.wait()

    def work(i, step, j):
        block = lax.rem(z + nr - step, nr)
        if step > 0:
            ring(j, step).wait_recv()
            if step < nr - 1:
                ring(j, step + 1).start()

        def read():
            if step > 0:
                return cols[j, step - 1].reshape(2 * m, gv.shape[1])
            return jnp.concatenate([gv[pl.ds(pl.multiple_of(h * sub + j * m, m), m)] for h in range(2)], axis=0)

        def gram(t, _):
            here = pl.ds(pl.multiple_of(t * tile, tile), tile)
            both = lax.dot_general(gv[here], read(), NT, preferred_element_type=jnp.float32).astype(jnp.bfloat16)
            part[i, 0, here] = both[:, :m]
            part[i, 1, here] = both[:, m:]
            return 0

        lax.fori_loop(0, rows // tile, gram, 0)
        swap(i).start()
        for h in range(2):
            weights(i, step, j, h).wait()

        def precondition(t, _):
            here = pl.ds(pl.multiple_of(t * tile, tile), tile)
            acc[here] += jnp.dot(rbuf[i, here], read(), preferred_element_type=jnp.float32)
            return 0

        lax.fori_loop(0, rows // tile, precondition, 0)

        @pl.when(j + 1 < chunks)
        def _():
            for h in range(2):
                weights(i, step, j + 1, h).start()

        swap(i).wait()

        def add(t, _):
            here = pl.ds(pl.multiple_of(t * tile, tile), tile)
            value = part[i, k, here].astype(jnp.float32) + got[i, here].astype(jnp.float32)
            return here, value.astype(jnp.bfloat16)

        @pl.when(block == q)
        def _():
            def keep(t, _):
                here, value = add(t, 0)
                heap[j, q, here] = value
                return 0

            lax.fori_loop(0, rows // tile, keep, 0)

        @pl.when(block != q)
        def _():
            @pl.when(j > 0)
            def _():
                spread(i, step, j - 1).wait_send()

            def give(t, _):
                here, value = add(t, 0)
                pair[i, here] = value
                return 0

            lax.fori_loop(0, rows // tile, give, 0)
            spread(i, step, j).start()

    def finish(j):
        for i in range(nq):
            @pl.when(i != q)
            def _():
                pltpu.make_async_remote_copy(
                    src_ref=pair.at[0], dst_ref=heap.at[j, i], send_sem=ss.at[0], recv_sem=sr.at[j, i],
                    device_id=(z, mate), device_id_type=MESH).wait_recv()

        @pl.when(j >= 2)
        def _():
            store(j - 2).wait()

        def total(t, _):
            here = pl.ds(pl.multiple_of(t * tile, tile), tile)
            value = heap[j, 0, here].astype(jnp.float32)
            for i in range(1, nq):
                value += heap[j, i, here].astype(jnp.float32)
            stage[j % 2, here] = value.astype(jnp.bfloat16)
            return 0

        lax.fori_loop(0, rows // tile, total, 0)
        store(j).start()

    def round_of(j, _):
        @pl.when((j >= 1) & (j + 1 < chunks))
        def _():
            ring(j + 1, 1).start()

        for i, (step, lag) in enumerate(units):
            @pl.when((j >= lag) & (j - lag < chunks))
            def _():
                work(i, step, j - lag)

        @pl.when(j >= 3)
        def _():
            finish(j - 3)

        return 0

    lax.fori_loop(0, chunks + 2, round_of, 0)

    def cast(t, _):
        here = pl.ds(pl.multiple_of(t * tile, tile), tile)
        gv[here] = acc[here].astype(jnp.bfloat16)
        return 0

    lax.fori_loop(0, rows // tile, cast, 0)
    result = pltpu.make_async_copy(gv, out_ref, ls.at[0])
    result.start()
    finish(chunks - 1)
    result.wait()
    if chunks > 1:
        store(chunks - 2).wait()
    store(chunks - 1).wait()
    for i, (step, _) in enumerate(units):
        @pl.when(lax.rem(z + nr - step, nr) != q)
        def _():
            spread(i, step, chunks - 1).wait_send()

    def drain(j, _):
        for step in range(1, nr):
            ring(j, step).wait_send()
        return 0

    lax.fori_loop(0, chunks, drain, 0)


def on_device(nr, nc, gradient, stat_old, inv_root):
    rows, lat = gradient.shape
    sub, m = rows // 2, WIDE
    chunks, nq = sub // m, nc // 2
    tile = min(512, rows)
    dma = pltpu.SemaphoreType.DMA
    half = jnp.bfloat16
    share, product = pl.pallas_call(
        functools.partial(kernel, nr, nc, m, tile),
        out_shape=(
            jax.ShapeDtypeStruct((rows, sub), half),
            jax.ShapeDtypeStruct((rows, lat), half),
        ),
        in_specs=[pl.BlockSpec(memory_space=pl.ANY)] * 2,
        out_specs=(pl.BlockSpec(memory_space=pl.ANY),) * 2,
        scratch_shapes=[
            pltpu.VMEM((rows, lat), half),
            pltpu.VMEM((rows, lat), jnp.float32),
            pltpu.VMEM((chunks, nr - 1, 2, m, lat), half),
            pltpu.VMEM((nr, rows, 2 * m), half),
            pltpu.VMEM((nr, 2, rows, m), half),
            pltpu.VMEM((nr, rows, m), half),
            pltpu.VMEM((nr, rows, m), half),
            pltpu.VMEM((chunks, nq, rows, m), half),
            pltpu.VMEM((2, rows, m), half),
            dma((chunks, nr - 1)),
            dma((chunks, nr - 1)),
            dma((nr, 2)),
            dma((nr,)),
            dma((nr,)),
            dma((nr,)),
            dma((chunks, nq)),
            dma((2,)),
            dma((2,)),
        ],
        compiler_params=pltpu.CompilerParams(
            collective_id=0, has_side_effects=True, vmem_limit_bytes=60 * 2**20
        ),
        cost_estimate=pl.CostEstimate(
            flops=4 * rows * lat * nr * rows, bytes_accessed=2 * rows * (2 * lat + sub + nr * rows), transcendentals=0
        ),
    )(gradient.reshape(2, sub, lat), inv_root)
    stat_new = 0.9 * stat_old + 0.1 * share.astype(jnp.float32)
    return stat_new, product


def solution(mesh):
    nr, nc = mesh.shape["row"], mesh.shape["col"]
    placed = (P("row", "col"), P("row", "col"), P("row", None))
    return jax.shard_map(
        functools.partial(on_device, nr, nc),
        mesh=mesh,
        in_specs=placed,
        out_specs=(P("row", "col"), P("row", "col")),
        check_vma=False,
    )
```

time: 574 us -> 322 us (0.56)
  waiting for transfers between devices: 435 us -> 0 us
  Pallas kernels: 0 us -> 309 us
  matrix products: 94.1 us -> 0 us
  local copies, waits for them, and re-layouts: 18.8 us -> 2.02 us
  between operations: 14 us -> 0.65 us
    pallas_call x0 -> x1, Pallas kernels: none -> 309 us  [on_device(): pl.pallas_call(functools.partial(kernel, nr, nc, m, tile), out_shape=(jax...]
    all_gather x1 -> x0, waiting for transfers between devices: 290 us -> none  [on_device(): columns = lax.all_gather(gradient, 'row', axis=0, tiled=True)]
    reduce_scatter x1 -> x0, waiting for transfers between devices: 145 us -> none  [on_device(): lax.psum_scatter(lax.dot_general(columns, gradient, (((1,), (1,)), ((), (...]
    dot_general x2 -> x0, matrix products: 94.1 us -> none  [the longest x1 48.9 us: on_device(): product = jnp.dot(inv_root, columns, preferred_element_type=jnp.float32)]
    unnamed x2 -> x3, local copies, waits for them, and re-layouts: 18.8 us -> 2.02 us
  transfers between devices with their start and end apart: 2 -> 0, of which waited for: 2 -> 0; matrix products, arithmetic and copies ran while one was open for 10% -> 0% of each run, Pallas kernels for 0% -> 0%
where the time goes in v1:
time: 322 us
  Pallas kernels  309 us (96%)
  other arithmetic  10.4 us (3%)
    pallas_call x1, Pallas kernels, on_device(): pl.pallas_call(functools.partial(kernel, nr, nc, m, tile), out_shape=(jax...  309 us
    add x1, other arithmetic, on_device(): stat_new = 0.9 * stat_old + 0.1 * share.astype(jnp.float32)  10.4 us

profile of v1, /device:TPU:2, one launch (start us, length us, event | category | flops | bytes accessed | tf_op | source)
XLA Modules:
  0.0 321.7 jit_solution(8065002694396231097)
XLA Ops:
  0.6 308.6 %shard_map.50 = (bf16[2048,1024]{1,0:T(8,128)(2,1)}, bf16[2048,1024]{1,0:T(8,128)(2,1)}) custom-call(bf16[2,1024,1024]{2,1,0:T(8,128)(2,1)} %bitcast.1, bf16[2048,8192]{1,0:T(8,128)(2,1)} %r_ref.1), custom_call_target="tpu_custom_call" | custom-call | flops 68719476736 | bytes 46137344 | tf_op jit(solution)/shard_map/pallas_call | solution.py:230
  309.2 0.0 copy-start
  309.2 10.4 %multiply_add_fusion = f32[2048,1024]{1,0:T(8,128)} fusion(bf16[2048,1024]{1,0:T(8,128)(2,1)} %get-tuple-element.4, f32[2048,1024]{1,0:T(8,128)} %param.4), kind=kLoop, calls=%fused_computation | loop fusion | flops 8388608 | bytes 20971520 | tf_op jit(solution)/shard_map/add | solution.py:265
  319.6 0.0 copy-done
  319.6 2.0 copy.6
Async XLA Ops:
  309.2 10.4 %copy-start = (bf16[2048,1024]{1,0:T(8,128)(2,1)S(1)}, bf16[2048,1024]{1,0:T(8,128)(2,1)}, u32[]{:S(2)}) copy-start(bf16[2048,1024]{1,0:T(8,128)(2,1)} %get-tuple-element.9) | copy-start | bytes 12582916

commit v2 on v1

v2 whole, which is shorter than its diff:
```python
import functools

import jax
import jax.numpy as jnp
from jax import lax
from jax.experimental import pallas as pl
from jax.experimental.pallas import tpu as pltpu
from jax.sharding import PartitionSpec as P

MESH = pl.DeviceIdType.MESH
WIDE = 128
NT = (((1,), (1,)), ((), ()))


def kernel(nr, nc, m, tile, g_ref, old_ref, r_ref, new_ref, out_ref, gv, acc, cols, rbuf, part, got, pair, heap, stat,
           zs, zr, rs, ps, pr, ss, sr, os, ns, ls):
    rows = gv.shape[0]
    sub = rows // 2
    chunks = sub // m
    nq = nc // 2
    z, c = lax.axis_index("row"), lax.axis_index("col")
    q, k = c // 2, c % 2
    odd = (q // 2 + q) % 2
    onward = 1 + (nr - 2) * odd
    back = nr - onward
    right, left = lax.rem(z + onward, nr), lax.rem(z + back, nr)
    mate = 2 * q + (1 - k)

    barrier = pltpu.get_barrier_semaphore()
    others = [(right, c), (left, c), (z, mate)]
    others += [(z, 2 * lax.rem(q + i, nq) + k) for i in range(1, nq)]
    for other in others:
        pl.semaphore_signal(barrier, inc=1, device_id=other, device_id_type=MESH)
    pl.semaphore_wait(barrier, len(others))

    def at(j):
        return pl.ds(pl.multiple_of(j * m, m), m)

    def ring(j, step):
        src = g_ref.at[:, at(j)] if step == 1 else cols.at[j, step - 2]
        return pltpu.make_async_remote_copy(
            src_ref=src, dst_ref=cols.at[j, step - 1], send_sem=zs.at[j, step - 1], recv_sem=zr.at[j, step - 1],
            device_id=(right, c), device_id_type=MESH)

    def weights(i, step, j, h):
        block = lax.rem(z + back * step, nr)
        first = pl.multiple_of((2 * block + h) * sub + j * m, m)
        return pltpu.make_async_copy(
            r_ref.at[:, pl.ds(first, m)], rbuf.at[i, :, pl.ds(h * m, m)], rs.at[i, h])

    def swap(i, j):
        return pltpu.make_async_remote_copy(
            src_ref=part.at[1 - k], dst_ref=got.at[j % 2, i], send_sem=ps.at[i], recv_sem=pr.at[j % 2, i],
            device_id=(z, mate), device_id_type=MESH)

    def spread(i, step, j):
        block = lax.rem(z + back * step, nr)
        return pltpu.make_async_remote_copy(
            src_ref=pair.at[i], dst_ref=heap.at[j, q], send_sem=ss.at[i], recv_sem=sr.at[j, q],
            device_id=(z, 2 * block + k), device_id_type=MESH)

    def load(j):
        return pltpu.make_async_copy(old_ref.at[:, at(j)], stat.at[j % 2], os.at[j % 2])

    def store(j):
        return pltpu.make_async_copy(stat.at[j % 2], new_ref.at[:, at(j)], ns.at[j % 2])

    ring(0, 1).start()
    whole = [pltpu.make_async_copy(g_ref.at[h], gv.at[pl.ds(h * sub, sub)], ls.at[h]) for h in range(2)]
    for copy in whole:
        copy.start()
    for step in range(nr):
        for h in range(2):
            weights(step, step, 0, h).start()
    load(0).start()

    def clear(t, _):
        acc[pl.ds(pl.multiple_of(t * tile, tile), tile)] = jnp.zeros((tile, acc.shape[1]), jnp.float32)
        return 0

    lax.fori_loop(0, rows // tile, clear, 0)
    for copy in whole:
        copy.wait()

    def work(i, step, j):
        block = lax.rem(z + back * step, nr)
        def read():
            if step > 0:
                return cols[j, step - 1].reshape(2 * m, gv.shape[1])
            return jnp.concatenate([gv[pl.ds(pl.multiple_of(h * sub + j * m, m), m)] for h in range(2)], axis=0)

        def gram(t, _):
            here = pl.ds(pl.multiple_of(t * tile, tile), tile)
            both = lax.dot_general(gv[here], read(), NT, preferred_element_type=jnp.float32).astype(jnp.bfloat16)
            part[0, here] = both[:, :m]
            part[1, here] = both[:, m:]
            return 0

        lax.fori_loop(0, rows // tile, gram, 0)
        swap(i, j).start()
        def multiply():
            for h in range(2):
                weights(i, step, j, h).wait()

            def precondition(t, _):
                here = pl.ds(pl.multiple_of(t * tile, tile), tile)
                acc[here] += jnp.dot(rbuf[i, here], read(), preferred_element_type=jnp.float32)
                return 0

            lax.fori_loop(0, rows // tile, precondition, 0)

            @pl.when(j + 1 < chunks)
            def _():
                for h in range(2):
                    weights(i, step, j + 1, h).start()

        if step < nr - 1:
            multiply()
        swap(i, j).wait()

        def add(t, _):
            here = pl.ds(pl.multiple_of(t * tile, tile), tile)
            value = part[k, here].astype(jnp.float32) + got[j % 2, i, here].astype(jnp.float32)
            return here, value.astype(jnp.bfloat16)

        @pl.when(block == q)
        def _():
            def keep(t, _):
                here, value = add(t, 0)
                heap[j, q, here] = value
                return 0

            lax.fori_loop(0, rows // tile, keep, 0)

        @pl.when(block != q)
        def _():
            @pl.when(j > 0)
            def _():
                spread(i, step, j - 1).wait_send()

            def give(t, _):
                here, value = add(t, 0)
                pair[i, here] = value
                return 0

            lax.fori_loop(0, rows // tile, give, 0)
            spread(i, step, j).start()

        if step == nr - 1:
            multiply()

    def finish(j):
        for i in range(nq):
            @pl.when(i != q)
            def _():
                pltpu.make_async_remote_copy(
                    src_ref=pair.at[0], dst_ref=heap.at[j, i], send_sem=ss.at[0], recv_sem=sr.at[j, i],
                    device_id=(z, mate), device_id_type=MESH).wait_recv()

        load(j).wait()

        def total(t, _):
            here = pl.ds(pl.multiple_of(t * tile, tile), tile)
            value = heap[j, 0, here].astype(jnp.float32)
            for i in range(1, nq):
                value += heap[j, i, here].astype(jnp.float32)
            stat[j % 2, here] = 0.9 * stat[j % 2, here] + 0.1 * value
            return 0

        lax.fori_loop(0, rows // tile, total, 0)
        store(j).start()

        @pl.when(j > 0)
        def _():
            store(j - 1).wait()

        @pl.when(j + 1 < chunks)
        def _():
            load(j + 1).start()

    def round_of(j, _):
        @pl.when(j + 1 < chunks)
        def _():
            ring(j + 1, 1).start()

        for step in range(1, nr):
            late = j - step + 1

            @pl.when((late >= 0) & (late < chunks))
            def _():
                if step < nr - 1:
                    ring(late, step).wait_recv()
                    ring(late, step + 1).start()

        for step in range(nr):
            late = j - max(step - 1, 0)

            @pl.when((late >= 0) & (late < chunks))
            def _():
                if step == nr - 1:
                    ring(late, step).wait_recv()
                work(step, step, late)

        @pl.when(j >= nr - 1)
        def _():
            finish(j - nr + 1)

        return 0

    lax.fori_loop(0, chunks + nr - 2, round_of, 0)

    def cast(t, _):
        here = pl.ds(pl.multiple_of(t * tile, tile), tile)
        gv[here] = acc[here].astype(jnp.bfloat16)
        return 0

    lax.fori_loop(0, rows // tile, cast, 0)
    result = pltpu.make_async_copy(gv, out_ref, ls.at[0])
    result.start()
    finish(chunks - 1)
    result.wait()
    store(chunks - 1).wait()
    for step in range(nr):
        @pl.when(lax.rem(z + back * step, nr) != q)
        def _():
            spread(step, step, chunks - 1).wait_send()

    def drain(j, _):
        for step in range(1, nr):
            ring(j, step).wait_send()
        return 0

    lax.fori_loop(0, chunks, drain, 0)


def on_device(nr, nc, gradient, stat_old, inv_root):
    rows, lat = gradient.shape
    sub, m = rows // 2, WIDE
    chunks, nq = sub // m, nc // 2
    tile = min(512, rows)
    dma = pltpu.SemaphoreType.DMA
    half = jnp.bfloat16
    return pl.pallas_call(
        functools.partial(kernel, nr, nc, m, tile),
        out_shape=(
            jax.ShapeDtypeStruct((rows, sub), jnp.float32),
            jax.ShapeDtypeStruct((rows, lat), half),
        ),
        in_specs=[pl.BlockSpec(memory_space=pl.ANY)] * 3,
        out_specs=(pl.BlockSpec(memory_space=pl.ANY),) * 2,
        scratch_shapes=[
            pltpu.VMEM((rows, lat), half),
            pltpu.VMEM((rows, lat), jnp.float32),
            pltpu.VMEM((chunks, nr - 1, 2, m, lat), half),
            pltpu.VMEM((nr, rows, 2 * m), half),
            pltpu.VMEM((2, rows, m), half),
            pltpu.VMEM((2, nr, rows, m), half),
            pltpu.VMEM((nr, rows, m), half),
            pltpu.VMEM((chunks, nq, rows, m), half),
            pltpu.VMEM((2, rows, m), jnp.float32),
            dma((chunks, nr - 1)),
            dma((chunks, nr - 1)),
            dma((nr, 2)),
            dma((nr,)),
            dma((2, nr)),
            dma((nr,)),
            dma((chunks, nq)),
            dma((2,)),
            dma((2,)),
            dma((2,)),
        ],
        compiler_params=pltpu.CompilerParams(
            collective_id=0, has_side_effects=True, vmem_limit_bytes=60 * 2**20
        ),
        cost_estimate=pl.CostEstimate(
            flops=4 * rows * lat * nr * rows, bytes_accessed=2 * rows * (2 * lat + 4 * sub + nr * rows), transcendentals=0
        ),
    )(gradient.reshape(2, sub, lat), stat_old, inv_root)


def solution(mesh):
    nr, nc = mesh.shape["row"], mesh.shape["col"]
    placed = (P("row", "col"), P("row", "col"), P("row", None))
    return jax.shard_map(
        functools.partial(on_device, nr, nc),
        mesh=mesh,
        in_specs=placed,
        out_specs=(P("row", "col"), P("row", "col")),
        check_vma=False,
    )
```

time: 322 us -> 320 us (level)
  other arithmetic: 10.4 us -> 0 us
  local copies, waits for them, and re-layouts: 2.02 us -> 10.6 us
    add x1 -> x0, other arithmetic: 10.4 us -> none  [on_device(): stat_new = 0.9 * stat_old + 0.1 * share.astype(jnp.float32)]
    unnamed x3 -> x4, local copies, waits for them, and re-layouts: 2.02 us -> 10.6 us
where the time goes in v2:
time: 320 us
  Pallas kernels  309 us (97%)
  local copies, waits for them, and re-layouts  10.6 us (3%)
    pallas_call x1, Pallas kernels, on_device(): pl.pallas_call(functools.partial(kernel, nr, nc, m, tile), out_shape=(jax...  309 us
    unnamed x4, local copies, waits for them, and re-layouts  10.6 us

profile of v2, /device:TPU:2, one launch (start us, length us, event | category | flops | bytes accessed | tf_op | source)
XLA Modules:
  0.0 320.2 jit_solution(2490543004898993449)
XLA Ops:
  0.6 309.0 %shard_map.50 = (f32[2048,1024]{1,0:T(8,128)}, bf16[2048,1024]{1,0:T(8,128)(2,1)}) custom-call(bf16[2,1024,1024]{2,1,0:T(8,128)(2,1)} %bitcast.1, f32[2048,1024]{1,0:T(8,128)} %old_ref.1, bf16[2048,8192]{1,0:T(8,128)(2,1)} %r_ref.1), custom_call_target="tpu_custom_call" | custom-call | flops 68719476736 | bytes 58720256 | tf_op jit(solution)/shard_map/pallas_call | solution.py:243
  309.6 0.0 copy-start
  309.6 8.6 %copy.7 = f32[2048,1024]{1,0:T(8,128)} copy(f32[2048,1024]{1,0:T(8,128)} %get-tuple-element.4) | data formatting | bytes 16777216
  318.2 0.0 copy-done
  318.2 2.0 copy.8
Async XLA Ops:
  309.6 8.6 %copy-start = (bf16[2048,1024]{1,0:T(8,128)(2,1)S(1)}, bf16[2048,1024]{1,0:T(8,128)(2,1)}, u32[]{:S(2)}) copy-start(bf16[2048,1024]{1,0:T(8,128)(2,1)} %get-tuple-element.5) | copy-start | bytes 12582916

commit v3 on v2

--- a/solution.py
+++ b/solution.py
@@ -12,19 +12,27 @@
 NT = (((1,), (1,)), ((), ()))
 
 
-def kernel(nr, nc, m, tile, g_ref, old_ref, r_ref, new_ref, out_ref, gv, acc, cols, rbuf, part, got, pair, heap, stat,
-           zs, zr, rs, ps, pr, ss, sr, os, ns, ls):
+def kernel(nr, nc, m, tile, g_ref, old_ref, r_ref, new_ref, out_ref, gv, acc, cols, rbuf, part, got, pair, relay, heap, stat,
+           zs, zr, rs, ps, pr, ss, ar, sr, os, ns, ls):
     rows = gv.shape[0]
     sub = rows // 2
     chunks = sub // m
     nq = nc // 2
     z, c = lax.axis_index("row"), lax.axis_index("col")
     q, k = c // 2, c % 2
-    odd = (q // 2 + q) % 2
-    onward = 1 + (nr - 2) * odd
-    back = nr - onward
-    right, left = lax.rem(z + onward, nr), lax.rem(z + back, nr)
+    back = nr - 1
+    right, left = lax.rem(z + 1, nr), lax.rem(z + back, nr)
     mate = 2 * q + (1 - k)
+
+    half = nq // 2
+
+    def digit(chip):
+        return (1 - k) * (chip % 2) + k * (chip // half)
+
+    def rest(chip):
+        return (1 - k) * (chip // 2) + k * (chip % half)
+
+    across = q + (1 - 2 * digit(q)) * ((1 - k) + k * half)
 
     barrier = pltpu.get_barrier_semaphore()
     others = [(right, c), (left, c), (z, mate)]
@@ -53,10 +61,16 @@
             src_ref=part.at[1 - k], dst_ref=got.at[j % 2, i], send_sem=ps.at[i], recv_sem=pr.at[j % 2, i],
             device_id=(z, mate), device_id_type=MESH)
 
+    def hand(i, step, j):
+        place = rest(lax.rem(z + back * step, nr))
+        return pltpu.make_async_remote_copy(
+            src_ref=pair.at[i], dst_ref=relay.at[j, place], send_sem=ss.at[i], recv_sem=ar.at[j, place],
+            device_id=(z, 2 * across + k), device_id_type=MESH)
+
     def spread(i, step, j):
         block = lax.rem(z + back * step, nr)
         return pltpu.make_async_remote_copy(
-            src_ref=pair.at[i], dst_ref=heap.at[j, q], send_sem=ss.at[i], recv_sem=sr.at[j, q],
+            src_ref=pair.at[i], dst_ref=heap.at[j, rest(q)], send_sem=ss.at[i], recv_sem=sr.at[j, rest(q)],
             device_id=(z, 2 * block + k), device_id_type=MESH)
 
     def load(j):
@@ -84,6 +98,7 @@
 
     def work(i, step, j):
         block = lax.rem(z + back * step, nr)
+
         def read():
             if step > 0:
                 return cols[j, step - 1].reshape(2 * m, gv.shape[1])
@@ -98,6 +113,7 @@
 
         lax.fori_loop(0, rows // tile, gram, 0)
         swap(i, j).start()
+
         def multiply():
             for h in range(2):
                 weights(i, step, j, h).wait()
@@ -118,40 +134,71 @@
             multiply()
         swap(i, j).wait()
 
+        @pl.when(j > 0)
+        def _():
+            sent(i, step, j - 1)
+
         def add(t, _):
             here = pl.ds(pl.multiple_of(t * tile, tile), tile)
             value = part[k, here].astype(jnp.float32) + got[j % 2, i, here].astype(jnp.float32)
+            pair[i, here] = value.astype(jnp.bfloat16)
+            return 0
+
+        lax.fori_loop(0, rows // tile, add, 0)
+
+        @pl.when(digit(block) != digit(q))
+        def _():
+            hand(i, step, j).start()
+
+        if step == nr - 1:
+            multiply()
+
+    def sent(i, step, j):
+        block = lax.rem(z + back * step, nr)
+
+        @pl.when(digit(block) != digit(q))
+        def _():
+            hand(i, step, j).wait_send()
+
+        @pl.when((digit(block) == digit(q)) & (block != q))
+        def _():
+            spread(i, step, j).wait_send()
+
+    def settle(i, step, j):
+        block = lax.rem(z + back * step, nr)
+
+        def add(t):
+            here = pl.ds(pl.multiple_of(t * tile, tile), tile)
+            value = pair[i, here].astype(jnp.float32) + relay[j, rest(q), here].astype(jnp.float32)
             return here, value.astype(jnp.bfloat16)
 
         @pl.when(block == q)
         def _():
+            hand(i, step, j).wait_recv()
+
             def keep(t, _):
-                here, value = add(t, 0)
-                heap[j, q, here] = value
+                here, value = add(t)
+                heap[j, rest(q), here] = value
                 return 0
 
             lax.fori_loop(0, rows // tile, keep, 0)
 
-        @pl.when(block != q)
-        def _():
-            @pl.when(j > 0)
-            def _():
-                spread(i, step, j - 1).wait_send()
+        @pl.when((digit(block) == digit(q)) & (block != q))
+        def _():
+            hand(i, step, j).wait_recv()
 
             def give(t, _):
-                here, value = add(t, 0)
-                pair[i, here] = value
+                here = pl.ds(pl.multiple_of(t * tile, tile), tile)
+                value = pair[i, here].astype(jnp.float32) + relay[j, rest(block), here].astype(jnp.float32)
+                pair[i, here] = value.astype(jnp.bfloat16)
                 return 0
 
             lax.fori_loop(0, rows // tile, give, 0)
             spread(i, step, j).start()
 
-        if step == nr - 1:
-            multiply()
-
     def finish(j):
-        for i in range(nq):
-            @pl.when(i != q)
+        for i in range(half):
+            @pl.when(i != rest(q))
             def _():
                 pltpu.make_async_remote_copy(
                     src_ref=pair.at[0], dst_ref=heap.at[j, i], send_sem=ss.at[0], recv_sem=sr.at[j, i],
@@ -162,7 +209,7 @@
         def total(t, _):
             here = pl.ds(pl.multiple_of(t * tile, tile), tile)
             value = heap[j, 0, here].astype(jnp.float32)
-            for i in range(1, nq):
+            for i in range(1, half):
                 value += heap[j, i, here].astype(jnp.float32)
             stat[j % 2, here] = 0.9 * stat[j % 2, here] + 0.1 * value
             return 0
@@ -201,6 +248,13 @@
                     ring(late, step).wait_recv()
                 work(step, step, late)
 
+            last = (step + nr - 1) % nr
+            before = j - (nr - 1) if step == 0 else j - max(last - 1, 0)
+
+            @pl.when((before >= 0) & (before < chunks))
+            def _():
+                settle(last, last, before)
+
         @pl.when(j >= nr - 1)
         def _():
             finish(j - nr + 1)
@@ -208,6 +262,8 @@
         return 0
 
     lax.fori_loop(0, chunks + nr - 2, round_of, 0)
+
+    settle(nr - 1, nr - 1, chunks - 1)
 
     def cast(t, _):
         here = pl.ds(pl.multiple_of(t * tile, tile), tile)
@@ -221,9 +277,7 @@
     result.wait()
     store(chunks - 1).wait()
     for step in range(nr):
-        @pl.when(lax.rem(z + back * step, nr) != q)
-        def _():
-            spread(step, step, chunks - 1).wait_send()
+        sent(step, step, chunks - 1)
 
     def drain(j, _):
         for step in range(1, nr):
@@ -256,7 +310,8 @@
             pltpu.VMEM((2, rows, m), half),
             pltpu.VMEM((2, nr, rows, m), half),
             pltpu.VMEM((nr, rows, m), half),
-            pltpu.VMEM((chunks, nq, rows, m), half),
+            pltpu.VMEM((chunks, nq // 2, rows, m), half),
+            pltpu.VMEM((chunks, nq // 2, rows, m), half),
             pltpu.VMEM((2, rows, m), jnp.float32),
             dma((chunks, nr - 1)),
             dma((chunks, nr - 1)),
@@ -264,7 +319,8 @@
             dma((nr,)),
             dma((2, nr)),
             dma((nr,)),
-            dma((chunks, nq)),
+            dma((chunks, nq // 2)),
+            dma((chunks, nq // 2)),
             dma((2,)),
             dma((2,)),
             dma((2,)),

time: 320 us -> 315 us (0.984)
  Pallas kernels: 309 us -> 302 us
    pallas_call x1, Pallas kernels: 309 us -> 302 us  [on_device(): pl.pallas_call(functools.partial(kernel, nr, nc, m, tile), out_shape=(jax...]
where the time goes in v3:
time: 315 us; the launch traced here: 313 us
  Pallas kernels  302 us (96%)
  local copies, waits for them, and re-layouts  10.6 us (3%)
    pallas_call x1, Pallas kernels, on_device(): pl.pallas_call(functools.partial(kernel, nr, nc, m, tile), out_shape=(jax...  302 us
    unnamed x4, local copies, waits for them, and re-layouts  10.6 us

profile of v3, /device:TPU:2, one launch (start us, length us, event | category | flops | bytes accessed | tf_op | source)
XLA Modules:
  0.0 313.1 jit_solution(14730926318687656462)
XLA Ops:
  0.6 301.8 %shard_map.50 = (f32[2048,1024]{1,0:T(8,128)}, bf16[2048,1024]{1,0:T(8,128)(2,1)}) custom-call(bf16[2,1024,1024]{2,1,0:T(8,128)(2,1)} %bitcast.1, f32[2048,1024]{1,0:T(8,128)} %old_ref.1, bf16[2048,8192]{1,0:T(8,128)(2,1)} %r_ref.1), custom_call_target="tpu_custom_call" | custom-call | flops 68719476736 | bytes 58720256 | tf_op jit(solution)/shard_map/pallas_call | solution.py:297
  302.4 0.0 copy-start
  302.4 8.6 %copy.7 = f32[2048,1024]{1,0:T(8,128)} copy(f32[2048,1024]{1,0:T(8,128)} %get-tuple-element.4) | data formatting | bytes 16777216
  311.0 0.0 copy-done
  311.0 2.0 copy.8
Async XLA Ops:
  302.4 8.6 %copy-start = (bf16[2048,1024]{1,0:T(8,128)(2,1)S(1)}, bf16[2048,1024]{1,0:T(8,128)(2,1)}, u32[]{:S(2)}) copy-start(bf16[2048,1024]{1,0:T(8,128)(2,1)} %get-tuple-element.5) | copy-start | bytes 12582916

commit v4 on v3

--- a/solution.py
+++ b/solution.py
@@ -16,6 +16,7 @@
            zs, zr, rs, ps, pr, ss, ar, sr, os, ns, ls):
     rows = gv.shape[0]
     sub = rows // 2
+    steps = rows // 2 // tile
     chunks = sub // m
     nq = nc // 2
     z, c = lax.axis_index("row"), lax.axis_index("col")
@@ -56,21 +57,27 @@
         return pltpu.make_async_copy(
             r_ref.at[:, pl.ds(first, m)], rbuf.at[i, :, pl.ds(h * m, m)], rs.at[i, h])
 
-    def swap(i, j):
+    def halves(p):
+        return pl.ds(p * (rows // 2), rows // 2)
+
+    def swap(i, j, p):
         return pltpu.make_async_remote_copy(
-            src_ref=part.at[1 - k], dst_ref=got.at[j % 2, i], send_sem=ps.at[i], recv_sem=pr.at[j % 2, i],
+            src_ref=part.at[1 - k, halves(p)], dst_ref=got.at[j % 2, i, halves(p)],
+            send_sem=ps.at[i, p], recv_sem=pr.at[j % 2, i, p],
             device_id=(z, mate), device_id_type=MESH)
 
-    def hand(i, step, j):
+    def hand(i, step, j, p):
         place = rest(lax.rem(z + back * step, nr))
         return pltpu.make_async_remote_copy(
-            src_ref=pair.at[i], dst_ref=relay.at[j, place], send_sem=ss.at[i], recv_sem=ar.at[j, place],
+            src_ref=pair.at[i, halves(p)], dst_ref=relay.at[j, place, halves(p)],
+            send_sem=ss.at[i, p], recv_sem=ar.at[j, place, p],
             device_id=(z, 2 * across + k), device_id_type=MESH)
 
-    def spread(i, step, j):
+    def spread(i, step, j, p):
         block = lax.rem(z + back * step, nr)
         return pltpu.make_async_remote_copy(
-            src_ref=pair.at[i], dst_ref=heap.at[j, rest(q)], send_sem=ss.at[i], recv_sem=sr.at[j, rest(q)],
+            src_ref=pair.at[i, halves(p)], dst_ref=heap.at[j, rest(q), halves(p)],
+            send_sem=ss.at[i, p], recv_sem=sr.at[j, rest(q), p],
             device_id=(z, 2 * block + k), device_id_type=MESH)
 
     def load(j):
@@ -111,8 +118,9 @@
             part[1, here] = both[:, m:]
             return 0
 
-        lax.fori_loop(0, rows // tile, gram, 0)
-        swap(i, j).start()
+        for p in range(2):
+            lax.fori_loop(p * steps, (p + 1) * steps, gram, 0)
+            swap(i, j, p).start()
 
         def multiply():
             for h in range(2):
@@ -132,7 +140,6 @@
 
         if step < nr - 1:
             multiply()
-        swap(i, j).wait()
 
         @pl.when(j > 0)
         def _():
@@ -144,11 +151,13 @@
             pair[i, here] = value.astype(jnp.bfloat16)
             return 0
 
-        lax.fori_loop(0, rows // tile, add, 0)
-
-        @pl.when(digit(block) != digit(q))
-        def _():
-            hand(i, step, j).start()
+        for p in range(2):
+            swap(i, j, p).wait()
+            lax.fori_loop(p * steps, (p + 1) * steps, add, 0)
+
+            @pl.when(digit(block) != digit(q))
+            def _():
+                hand(i, step, j, p).start()
 
         if step == nr - 1:
             multiply()
@@ -158,11 +167,13 @@
 
         @pl.when(digit(block) != digit(q))
         def _():
-            hand(i, step, j).wait_send()
+            for p in range(2):
+                hand(i, step, j, p).wait_send()
 
         @pl.when((digit(block) == digit(q)) & (block != q))
         def _():
-            spread(i, step, j).wait_send()
+            for p in range(2):
+                spread(i, step, j, p).wait_send()
 
     def settle(i, step, j):
         block = lax.rem(z + back * step, nr)
@@ -174,7 +185,8 @@
 
         @pl.when(block == q)
         def _():
-            hand(i, step, j).wait_recv()
+            for p in range(2):
+                hand(i, step, j, p).wait_recv()
 
             def keep(t, _):
                 here, value = add(t)
@@ -185,24 +197,26 @@
 
         @pl.when((digit(block) == digit(q)) & (block != q))
         def _():
-            hand(i, step, j).wait_recv()
-
             def give(t, _):
                 here = pl.ds(pl.multiple_of(t * tile, tile), tile)
                 value = pair[i, here].astype(jnp.float32) + relay[j, rest(block), here].astype(jnp.float32)
                 pair[i, here] = value.astype(jnp.bfloat16)
                 return 0
 
-            lax.fori_loop(0, rows // tile, give, 0)
-            spread(i, step, j).start()
+            for p in range(2):
+                hand(i, step, j, p).wait_recv()
+                lax.fori_loop(p * steps, (p + 1) * steps, give, 0)
+                spread(i, step, j, p).start()
 
     def finish(j):
         for i in range(half):
             @pl.when(i != rest(q))
             def _():
-                pltpu.make_async_remote_copy(
-                    src_ref=pair.at[0], dst_ref=heap.at[j, i], send_sem=ss.at[0], recv_sem=sr.at[j, i],
-                    device_id=(z, mate), device_id_type=MESH).wait_recv()
+                for p in range(2):
+                    pltpu.make_async_remote_copy(
+                        src_ref=pair.at[0, halves(p)], dst_ref=heap.at[j, i, halves(p)],
+                        send_sem=ss.at[0, p], recv_sem=sr.at[j, i, p],
+                        device_id=(z, mate), device_id_type=MESH).wait_recv()
 
         load(j).wait()
 
@@ -291,7 +305,7 @@
     rows, lat = gradient.shape
     sub, m = rows // 2, WIDE
     chunks, nq = sub // m, nc // 2
-    tile = min(512, rows)
+    tile = min(512, rows // 2)
     dma = pltpu.SemaphoreType.DMA
     half = jnp.bfloat16
     return pl.pallas_call(
@@ -316,11 +330,11 @@
             dma((chunks, nr - 1)),
             dma((chunks, nr - 1)),
             dma((nr, 2)),
-            dma((nr,)),
-            dma((2, nr)),
-            dma((nr,)),
-            dma((chunks, nq // 2)),
-            dma((chunks, nq // 2)),
+            dma((nr, 2)),
+            dma((2, nr, 2)),
+            dma((nr, 2)),
+            dma((chunks, nq // 2, 2)),
+            dma((chunks, nq // 2, 2)),
             dma((2,)),
             dma((2,)),
             dma((2,)),

time: 315 us -> 312 us (level)
  Pallas kernels: 302 us -> 296 us
    pallas_call x1, Pallas kernels: 302 us -> 296 us  [on_device(): pl.pallas_call(functools.partial(kernel, nr, nc, m, tile), out_shape=(jax...]
where the time goes in v4:
time: 312 us; the launch traced here: 307 us
  Pallas kernels  296 us (95%)
  local copies, waits for them, and re-layouts  10.6 us (3%)
    pallas_call x1, Pallas kernels, on_device(): pl.pallas_call(functools.partial(kernel, nr, nc, m, tile), out_shape=(jax...  296 us
    unnamed x4, local copies, waits for them, and re-layouts  10.6 us

profile of v4, /device:TPU:2, one launch (start us, length us, event | category | flops | bytes accessed | tf_op | source)
XLA Modules:
  0.0 307.4 jit_solution(260166478312196975)
XLA Ops:
  0.6 296.1 %shard_map.50 = (f32[2048,1024]{1,0:T(8,128)}, bf16[2048,1024]{1,0:T(8,128)(2,1)}) custom-call(bf16[2,1024,1024]{2,1,0:T(8,128)(2,1)} %bitcast.1, f32[2048,1024]{1,0:T(8,128)} %old_ref.1, bf16[2048,8192]{1,0:T(8,128)(2,1)} %r_ref.1), custom_call_target="tpu_custom_call" | custom-call | flops 68719476736 | bytes 58720256 | tf_op jit(solution)/shard_map/pallas_call | solution.py:311
  296.8 0.0 copy-start
  296.8 8.6 %copy.7 = f32[2048,1024]{1,0:T(8,128)} copy(f32[2048,1024]{1,0:T(8,128)} %get-tuple-element.4) | data formatting | bytes 16777216
  305.4 0.0 copy-done
  305.4 2.0 copy.8
Async XLA Ops:
  296.8 8.6 %copy-start = (bf16[2048,1024]{1,0:T(8,128)(2,1)S(1)}, bf16[2048,1024]{1,0:T(8,128)(2,1)}, u32[]{:S(2)}) copy-start(bf16[2048,1024]{1,0:T(8,128)(2,1)} %get-tuple-element.5) | copy-start | bytes 12582916
